TPU v7x, 32 devices: a whole 2x2x4 slice. The times are simulated.
32 devices in a mesh: replica: 4 (over x, core), shard: 8 (over z, y).
Axes of the slice: x: 2, y: 2, z: 4, core: 2. Of those that a mesh axis runs over, the one named last changes fastest.
Arguments:
- tokens: bfloat16 [32768, 768], P(('replica', 'shard')), may hold values from -6 to 6
- gain_attn: bfloat16 [768], P('shard'), may hold values from 0.099609375 to 1.8984375
- w_qkv: bfloat16 [768, 2304], P('shard'), may hold values from -0.3125 to 0.3125
- w_out: bfloat16 [768, 768], P('shard'), may hold values from -0.875 to 0.875
- gain_ffn: bfloat16 [768], P('shard'), may hold values from 0.099609375 to 1.8984375
- w_in: bfloat16 [768, 2304], P('shard'), may hold values from -0.21875 to 0.21875
- w_down: bfloat16 [1152, 768], P('shard'), may hold values from -0.1875 to 0.1875
- cotangent: bfloat16 [32768, 768], P(('replica', 'shard')), may hold values from -6 to 6
Outputs:
- output: bfloat16 [32768, 768], P(('replica', 'shard'))
- input_grad: bfloat16 [32768, 768], P(('replica', 'shard'))
- grad_gain_attn: float32 [768], P('shard')
- grad_qkv: float32 [768, 2304], P('shard')
- grad_out: float32 [768, 768], P('shard')
- grad_gain_ffn: float32 [768], P('shard')
- grad_in: float32 [768, 2304], P('shard')
- grad_down: float32 [1152, 768], P('shard')
All inputs are finite; a program needn't handle non-finite values.
Results may differ from a plain program's by a relative error of at most 0.018.
Values may be sent and summed in bfloat16 or wider, within the bound.
A program may use at most 128 MiB of HBM per device.

v0:
```python
import math
import jax
import jax.numpy as jnp
from jax import lax
from jax.sharding import PartitionSpec as P

D = 768
HEADS = 12
HEAD_DIM = 64
FF = 1152
WINDOW = 128
LENGTH = 1024
epsilon = 1e-05


def normalize(values):
    centre = values - jnp.mean(values, axis=-1, keepdims=True)
    inverse = lax.rsqrt(jnp.mean(centre * centre, axis=-1, keepdims=True) + epsilon)
    return (centre * inverse, inverse)


def norm_back(grad_norm, standard, inverse, gain):
    scaled = grad_norm * gain
    return inverse * (
        scaled
        - jnp.mean(scaled, axis=-1, keepdims=True)
        - standard * jnp.mean(scaled * standard, axis=-1, keepdims=True)
    )


def rotary_tables(count):
    half_dim = HEAD_DIM // 2
    freqs = 10000.0 ** (-(jnp.arange(half_dim, dtype=jnp.float32) * 2.0) / HEAD_DIM)
    places = (jnp.arange(count, dtype=jnp.int32) % LENGTH).astype(jnp.float32)
    angles = places[:, None] * freqs[None, :]
    angles = jnp.concatenate([angles, angles], axis=1)
    return (jnp.cos(angles)[:, None, :], jnp.sin(angles)[:, None, :])


def rotate_half(values):
    half_dim = values.shape[-1] // 2
    return jnp.concatenate([-values[..., half_dim:], values[..., :half_dim]], axis=-1)


def rotate_back(values):
    half_dim = values.shape[-1] // 2
    return jnp.concatenate([values[..., half_dim:], -values[..., :half_dim]], axis=-1)


def windows(field, block_rows, margin):
    seq_count = field.shape[0] // LENGTH
    blocks = LENGTH // block_rows
    shaped = field.reshape(seq_count, LENGTH, HEADS, HEAD_DIM)
    padded = jnp.pad(shaped, ((0, 0), (margin, block_rows - margin), (0, 0), (0, 0)))
    first = padded[:, :LENGTH].reshape(seq_count, blocks, block_rows, HEADS, HEAD_DIM)
    second = padded[:, block_rows : block_rows + LENGTH].reshape(
        seq_count, blocks, block_rows, HEADS, HEAD_DIM
    )
    joined = jnp.concatenate([first, second[:, :, : 2 * margin]], axis=2)
    return joined.reshape(seq_count * blocks, block_rows + 2 * margin, HEADS, HEAD_DIM)


def unwindow(field, block_rows, margin):
    blocks = LENGTH // block_rows
    seq_count = field.shape[0] // blocks
    shaped = field.reshape(seq_count, blocks, block_rows + 2 * margin, HEADS, HEAD_DIM)
    first = shaped[:, :, :block_rows].reshape(seq_count, LENGTH, HEADS, HEAD_DIM)
    second = jnp.pad(
        shaped[:, :, block_rows:], ((0, 0), (0, 0), (0, block_rows - 2 * margin), (0, 0), (0, 0))
    )
    second = second.reshape(seq_count, LENGTH, HEADS, HEAD_DIM)
    whole = jnp.pad(first, ((0, 0), (0, block_rows), (0, 0), (0, 0))) + jnp.pad(
        second, ((0, 0), (block_rows, 0), (0, 0), (0, 0))
    )
    return whole[:, margin : margin + LENGTH].reshape(seq_count * LENGTH, HEADS, HEAD_DIM)


def to_items(field):
    per_group = math.gcd(HEADS, 4)
    head_groups = HEADS // per_group
    count, rows = (field.shape[0], field.shape[1])
    shaped = field.reshape(count, rows, head_groups, per_group, HEAD_DIM).transpose(0, 2, 1, 3, 4)
    return shaped.reshape(count * head_groups, rows, per_group, HEAD_DIM)


def from_items(field):
    per_group = math.gcd(HEADS, 4)
    head_groups = HEADS // per_group
    count, rows = (field.shape[0] // head_groups, field.shape[1])
    shaped = field.reshape(count, head_groups, rows, per_group, HEAD_DIM).transpose(0, 2, 1, 3, 4)
    return shaped.reshape(count, rows, HEADS, HEAD_DIM)


def block_scores(query_part, key_part, start, block_rows, margin):
    span = key_part.shape[0]
    query_pos = start + jnp.arange(block_rows, dtype=jnp.int32)[:, None]
    key_pos = start - margin + jnp.arange(span, dtype=jnp.int32)[None, :]
    allowed = (key_pos >= 0) & (key_pos < LENGTH) & (jnp.abs(query_pos - key_pos) <= margin)
    raw = jnp.einsum(
        "qhd,khd->hqk", query_part, key_part, preferred_element_type=jnp.float32
    ) * HEAD_DIM ** (-0.5)
    return jnp.where(allowed[None], raw, -1e30)


def block_starts(count, block_rows):
    per_group = math.gcd(HEADS, 4)
    blocks = LENGTH // block_rows
    starts = jnp.arange(count, dtype=jnp.int32) % blocks * block_rows
    return jnp.repeat(starts, HEADS // per_group)


def attend_forward(queries, keys, values):
    count_tok = queries.shape[0]
    block_rows = min(512, LENGTH)
    margin = WINDOW // 2
    query_items = to_items(queries.reshape(count_tok // block_rows, block_rows, HEADS, HEAD_DIM))
    key_items = to_items(windows(keys, block_rows, margin))
    value_items = to_items(windows(values, block_rows, margin))
    starts = block_starts(count_tok // block_rows, block_rows)

    def one_block(pieces):
        query_part, key_part, value_part, start = pieces
        scores = block_scores(query_part, key_part, start, block_rows, margin)
        top = jnp.max(scores, axis=-1, keepdims=True)
        expo = jnp.exp(scores - top)
        total = jnp.sum(expo, axis=-1, keepdims=True)
        probs = (expo / total).astype(jnp.bfloat16)
        mixed = jnp.einsum("hqk,khd->qhd", probs, value_part, preferred_element_type=jnp.float32)
        return (mixed.astype(jnp.bfloat16), top[..., 0] + jnp.log(total[..., 0]))

    mixed, log_totals = lax.map(one_block, (query_items, key_items, value_items, starts))
    return (from_items(mixed).reshape(count_tok, D), log_totals)


def attend_backward(queries, keys, values, grad_mixed, log_totals):
    count_tok = queries.shape[0]
    block_rows = min(512, LENGTH)
    margin = WINDOW // 2
    scale = HEAD_DIM ** (-0.5)
    query_items = to_items(queries.reshape(count_tok // block_rows, block_rows, HEADS, HEAD_DIM))
    grad_items = to_items(grad_mixed.reshape(count_tok // block_rows, block_rows, HEADS, HEAD_DIM))
    key_items = to_items(windows(keys, block_rows, margin))
    value_items = to_items(windows(values, block_rows, margin))
    starts = block_starts(count_tok // block_rows, block_rows)

    def one_block(pieces):
        query_part, key_part, value_part, grad_part, log_part, start = pieces
        scores = block_scores(query_part, key_part, start, block_rows, margin)
        probs = jnp.exp(scores - log_part[..., None])
        grad_probs = jnp.einsum(
            "qhd,khd->hqk", grad_part, value_part, preferred_element_type=jnp.float32
        )
        centre = jnp.sum(grad_probs * probs, axis=-1, keepdims=True)
        grad_scores = (probs * (grad_probs - centre)).astype(jnp.bfloat16)
        grad_query = (
            jnp.einsum("hqk,khd->qhd", grad_scores, key_part, preferred_element_type=jnp.float32)
            * scale
        )
        grad_key = (
            jnp.einsum("hqk,qhd->khd", grad_scores, query_part, preferred_element_type=jnp.float32)
            * scale
        )
        grad_value = jnp.einsum(
            "hqk,qhd->khd",
            probs.astype(jnp.bfloat16),
            grad_part,
            preferred_element_type=jnp.float32,
        )
        return (grad_query, grad_key, grad_value)

    grad_query, grad_key, grad_value = lax.map(
        one_block, (query_items, key_items, value_items, grad_items, log_totals, starts)
    )
    grad_query = from_items(grad_query).reshape(count_tok, HEADS, HEAD_DIM)
    grad_key = unwindow(from_items(grad_key), block_rows, margin)
    grad_value = unwindow(from_items(grad_value), block_rows, margin)
    return (grad_query, grad_key, grad_value)


def body(tokens, gain_attn, w_qkv, w_out, gain_ffn, w_in, w_down, cotangent):
    count_tok = tokens.shape[0]
    gain_one, joint_weight, out_weight = (
        lax.all_gather(gain_attn, "shard", axis=0, tiled=True),
        lax.all_gather(w_qkv, "shard", axis=0, tiled=True),
        lax.all_gather(w_out, "shard", axis=0, tiled=True),
    )
    gain_two, in_weight, down_weight = (
        lax.all_gather(gain_ffn, "shard", axis=0, tiled=True),
        lax.all_gather(w_in, "shard", axis=0, tiled=True),
        lax.all_gather(w_down, "shard", axis=0, tiled=True),
    )
    stream = tokens.astype(jnp.float32)
    standard_one, inverse_one = normalize(stream)
    normed_attn = (standard_one * gain_one.astype(jnp.float32)).astype(jnp.bfloat16)
    projected = jnp.dot(normed_attn, joint_weight, preferred_element_type=jnp.float32)
    projected = projected.reshape(count_tok, 3, HEADS, HEAD_DIM)
    cosine, sine = rotary_tables(count_tok)
    raw_query = projected[:, 0]
    raw_key = projected[:, 1]
    queries = (raw_query * cosine + rotate_half(raw_query) * sine).astype(jnp.bfloat16)
    keys = (raw_key * cosine + rotate_half(raw_key) * sine).astype(jnp.bfloat16)
    values = projected[:, 2].astype(jnp.bfloat16)
    attended, log_totals = attend_forward(queries, keys, values)
    after_attn = stream + jnp.dot(attended, out_weight, preferred_element_type=jnp.float32)
    standard_two, inverse_two = normalize(after_attn)
    normed_ffn = (standard_two * gain_two.astype(jnp.float32)).astype(jnp.bfloat16)
    gate_up = jnp.dot(normed_ffn, in_weight, preferred_element_type=jnp.float32)
    lifted = gate_up[:, :FF]
    gate_part = gate_up[:, FF:]
    normal_cdf = 0.5 * (1.0 + lax.erf(lifted * 0.7071067811865476))
    gelu_value = lifted * normal_cdf
    activated = (gelu_value * gate_part).astype(jnp.bfloat16)
    final = after_attn + jnp.dot(activated, down_weight, preferred_element_type=jnp.float32)
    output = final.astype(jnp.bfloat16)
    gain_one, joint_weight, out_weight = (
        lax.all_gather(gain_attn, "shard", axis=0, tiled=True),
        lax.all_gather(w_qkv, "shard", axis=0, tiled=True),
        lax.all_gather(w_out, "shard", axis=0, tiled=True),
    )
    gain_two, in_weight, down_weight = (
        lax.all_gather(gain_ffn, "shard", axis=0, tiled=True),
        lax.all_gather(w_in, "shard", axis=0, tiled=True),
        lax.all_gather(w_down, "shard", axis=0, tiled=True),
    )
    grad_final = cotangent.astype(jnp.float32)
    grad_down = jnp.einsum("tf,td->fd", activated, cotangent, preferred_element_type=jnp.float32)
    grad_act = jnp.einsum("td,fd->tf", cotangent, down_weight, preferred_element_type=jnp.float32)
    density = jnp.exp(-0.5 * lifted * lifted) * 0.3989422804014327
    grad_lifted = grad_act * gate_part * (normal_cdf + lifted * density)
    grad_gate = grad_act * gelu_value
    grad_gate_up = jnp.concatenate([grad_lifted, grad_gate], axis=1).astype(jnp.bfloat16)
    grad_in = jnp.einsum("td,te->de", normed_ffn, grad_gate_up, preferred_element_type=jnp.float32)
    grad_norm_ffn = jnp.einsum(
        "te,de->td", grad_gate_up, in_weight, preferred_element_type=jnp.float32
    )
    grad_gain_ffn = jnp.sum(grad_norm_ffn * standard_two, axis=0)
    grad_after = grad_final + norm_back(
        grad_norm_ffn, standard_two, inverse_two, gain_two.astype(jnp.float32)
    )
    ffn_members = (grad_gain_ffn, grad_in, grad_down)
    owned_gain_ffn, owned_in, owned_down = (
        lax.psum_scatter(ffn_members[0], "shard", scatter_dimension=0, tiled=True),
        lax.psum_scatter(ffn_members[1], "shard", scatter_dimension=0, tiled=True),
        lax.psum_scatter(ffn_members[2], "shard", scatter_dimension=0, tiled=True),
    )
    grad_branch = grad_after.astype(jnp.bfloat16)
    grad_out = jnp.einsum("td,te->de", attended, grad_branch, preferred_element_type=jnp.float32)
    grad_attended = jnp.einsum(
        "te,de->td", grad_branch, out_weight, preferred_element_type=jnp.float32
    ).astype(jnp.bfloat16)
    grad_query, grad_key, grad_value = attend_backward(
        queries, keys, values, grad_attended, log_totals
    )
    grad_query = grad_query * cosine + rotate_back(grad_query * sine)
    grad_key = grad_key * cosine + rotate_back(grad_key * sine)
    grad_projected = jnp.stack([grad_query, grad_key, grad_value], axis=1)
    grad_projected = grad_projected.reshape(count_tok, 3 * D).astype(jnp.bfloat16)
    grad_qkv = jnp.einsum(
        "td,te->de", normed_attn, grad_projected, preferred_element_type=jnp.float32
    )
    grad_norm_attn = jnp.einsum(
        "te,de->td", grad_projected, joint_weight, preferred_element_type=jnp.float32
    )
    grad_gain_attn = jnp.sum(grad_norm_attn * standard_one, axis=0)
    input_grad = grad_after + norm_back(
        grad_norm_attn, standard_one, inverse_one, gain_one.astype(jnp.float32)
    )
    attn_members = (grad_gain_attn, grad_qkv, grad_out)
    owned_gain_attn, owned_qkv, owned_out = (
        lax.psum_scatter(attn_members[0], "shard", scatter_dimension=0, tiled=True),
        lax.psum_scatter(attn_members[1], "shard", scatter_dimension=0, tiled=True),
        lax.psum_scatter(attn_members[2], "shard", scatter_dimension=0, tiled=True),
    )
    summed = (
        lax.psum(owned_gain_attn.astype(jnp.bfloat16), "replica").astype(jnp.float32),
        lax.psum(owned_qkv.astype(jnp.bfloat16), "replica").astype(jnp.float32),
        lax.psum(owned_out.astype(jnp.bfloat16), "replica").astype(jnp.float32),
        lax.psum(owned_gain_ffn.astype(jnp.bfloat16), "replica").astype(jnp.float32),
        lax.psum(owned_in.astype(jnp.bfloat16), "replica").astype(jnp.float32),
        lax.psum(owned_down.astype(jnp.bfloat16), "replica").astype(jnp.float32),
    )
    return (
        output,
        input_grad.astype(jnp.bfloat16),
        summed[0],
        summed[1],
        summed[2],
        summed[3],
        summed[4],
        summed[5],
    )


def solution(mesh):
    return jax.shard_map(
        body,
        mesh=mesh,
        in_specs=(
            P(("replica", "shard"), None),
            P("shard"),
            P("shard", None),
            P("shard", None),
            P("shard"),
            P("shard", None),
            P("shard", None),
            P(("replica", "shard"), None),
        ),
        out_specs=(
            P(("replica", "shard"), None),
            P(("replica", "shard"), None),
            P("shard"),
            P("shard", None),
            P("shard", None),
            P("shard"),
            P("shard", None),
            P("shard", None),
        ),
        check_vma=False,
    )
```

profile of v0, /device:TPU:0, one launch (start us, length us, event | category | flops | bytes accessed | tf_op | source)
XLA Modules:
  0.0 722.2 jit_solution(9472683614992483625)
XLA Ops:
  14.4 23.5 %all-reduce.13 = (bf16[768]{0:T(1024)(128)(2,1)S(1)}, bf16[768]{0:T(1024)(128)(2,1)S(1)}) all-reduce(bf16[768]{0:T(1024)(128)(2,1)S(1)} %dynamic-update-slice, bf16[768]{0:T(1024)(128)(2,1)S(1)} %dynamic-update-slice.1), channel_id=1, replica_groups=mesh['replica'=4,'shard'=8] {'shard'}, use_global_device_ids=true, to_apply=%add.8 | all-reduce | flops 1536 | bytes 6144
  39.1 4.4 fusion.101
  46.5 31.9 %all-gather.5.cloned.1.call-done = bf16[768,2304]{1,0:T(8,128)(2,1)} async-done(((bf16[96,2304]{1,0:T(8,128)(2,1)}), bf16[768,2304]{1,0:T(8,128)(2,1)}) %all-gather.5.cloned.1.call-update) | async-done | bytes 3538960 | tf_op jit(solution)/shard_map/all_gather | solution.py:184
  78.4 6.0 fusion.96
  84.4 4.2 slice_bitcast_fusion
  93.5 3.9 reshape.520
  100.0 3.7 maximum_bitcast_fusion.1
  106.0 3.4 concatenate.91
  109.4 3.4 concatenate.92
  112.8 5.6 squeeze.70
  118.4 4.7 fusion.90
  127.8 3.9 reshape.516
  133.8 4.4 concatenate.87
  138.2 3.7 maximum_bitcast_fusion
  143.6 61.0 %while.30 = (s32[]{:T(128)}, bf16[6,512,4,64]{1,3,2,0:T(8,128)(2,1)}, f32[6,4,512]{2,1,0:T(4,128)}, bf16[6,640,4,64]{1,3,2,0:T(8,128)(2,1)}, s32[6]{0:T(128)S(1)...) while((s32[]{:T(128)}, ...), condition=%wide.region_5.6_spmd, body=%wide.region_2.5_spmd.sunk | while | flops 352716416 | bytes 18297728 | solution.py:131
  150.3 3.5 fusion.154
  160.4 3.5 fusion.154
  170.6 3.5 fusion.154
  180.7 3.5 fusion.154
  190.9 3.5 fusion.154
  201.0 3.5 fusion.154
  214.7 10.7 %fusion.110 = f32[1024,2304]{1,0:T(8,128)} fusion(bf16[768,2304]{1,0:T(8,128)(2,1)} %all-gather.9.cloned.1.call-done, f32[1024,768]{0,1:T(8,128)} %copy-done.4, f32[768]{0:T(1024)S(1)} %convert_element_type.164, f32[1024]{0:T(1024)S(1)} %add_rsqrt_fusion, f32[1024]{0:T(1024)S(1)} %broadcast_multiply_fusion.7), kind=kOutput, calls=%fused_computation.187 | convolution fusion | flops 3627024384 | bytes 16133120 | tf_op jit(solution)/shard_map/dot_general | solution.py:207
  225.4 7.5 %all-gather.11.cloned.1.call-done = bf16[1152,768]{1,0:T(8,128)(2,1)} async-done(((bf16[144,768]{1,0:T(8,128)(2,1)}), bf16[1152,768]{1,0:T(8,128)(2,1)}) %all-gather.11.cloned.1.call-update) | async-done | bytes 1769488 | tf_op jit(solution)/shard_map/all_gather | solution.py:190
  232.8 9.2 %fusion.61 = (bf16[1024,1152]{1,0:T(8,128)(2,1)S(1)}, bf16[1024,1152]{1,0:T(8,128)(2,1)S(1)}, bf16[1024,1152]{1,0:T(8,128)(2,1)}) fusion(f32[1024,2304]{1,0:T(8,128)} %fusion.110, bf16[1024,768]{1,0:T(8,128)(2,1)S(1)} %copy-done.20, bf16[1152,768]{1,0:T(8,128)(2,1)} %all-gather.11.cloned.1.call-done), kind=kOutput, calls=%fused_computation.78 | convolution fusion | flops 1830813696 | bytes 19857408 | tf_op jit(solution)/shard_map/td,fd->tf/dot_general | solution.py:227
  242.1 4.9 multiply_reduce_fusion.1
  252.6 5.5 fusion.113
  259.5 4.5 convolution_convert_fusion
  270.5 9.3 %fusion.83 = f32[768,2304]{1,0:T(8,128)} fusion(bf16[1024,1152]{1,0:T(8,128)(2,1)} %copy-done.36, bf16[1024,1152]{1,0:T(8,128)(2,1)} %copy-done.35, f32[1024,768]{0,1:T(8,128)S(1)} %copy-done.6, f32[768]{0:T(1024)S(1)} %convert_element_type.164, f32[1024]{0:T(1024)S(1)} %add_rsqrt_fusion, f32[1024]{0:T(1024)S(1)} %broadcast_multiply_fusion.7), kind=kOutput, calls=%fused_computation.123 | convolution fusion | flops 3636461568 | bytes 14953472 | tf_op jit(solution)/shard_map/td,te->de/dot_general | solution.py:232
  279.8 95.7 %while.31 = (s32[]{:T(128)}, f32[6,512,4,64]{1,3,2,0:T(8,128)}, f32[6,640,4,64]{1,3,2,0:T(8,128)}, f32[6,640,4,64]{1,3,2,0:T(8,128)}, bf16[6,640,4,64]{1,3,2,0:T...) while((s32[]{:T(128)}, f32[6,512,4,64]{1,3,2,0:T(8,128)}, ...), condition=%wide.region_12.13_spmd, body=%wide.region_10.12_spmd.sunk | while | flops 860128896 | bytes 44572060 | solution.py:171
  375.6 5.2 copy.70
  387.1 3.8 reshape_reshape.26
  390.9 4.0 reshape_reshape.25
  394.9 5.2 copy.71
  406.9 4.3 reshape.527
  411.2 5.6 reshape.526
  416.8 4.0 pad.36
  420.8 5.6 reshape.532
  426.4 6.0 reshape.531
  432.5 4.1 fusion.86
  445.9 6.2 fusion.94
  452.8 9.3 %fusion.74 = (f32[768]{0:T(1024)S(1)}, f32[1024]{0:T(1024)S(1)}, f32[1024]{0:T(1024)S(1)}, f32[1024,768]{0,1:T(8,128)}) fusion(bf16[1024,768]{0,1:T(8,128)(2,1)S(1)} %copy-done.2, f32[1024]{0:T(1024)S(1)} %copy-done.26, f32[1024]{0:T(1024)S(1)} %copy-done.24, f32[768]{0:T(1024)S(1)} %copy-done.28, bf16[768,2304]{1,0:T(8,128)(2,1)} %all-gather.5.cloned.1.call-done, ...), kind=kOutput, calls=%fused_computation.97 | convolution fusion | flops 3630953728 | bytes 12998656 | tf_op jit(solution)/shard_map/te,de->td/dot_general | solution.py:261
  462.1 20.3 %all-reduce.12 = (bf16[768]{0:T(1024)(128)(2,1)S(1)}, bf16[768]{0:T(1024)(128)(2,1)S(1)}) all-reduce(f32[768]{0:T(1024)S(1)} %get-tuple-element.264, f32[768]{0:T(1024)S(1)} %copy-done.29), channel_id=2, replica_groups=mesh['replica'=4,'shard'=8] {'shard'}, use_global_device_ids=true, to_apply=%region_16.17.clone | all-reduce | flops 1536 | bytes 9216
  482.6 6.2 all-reduce.14
  489.8 3.9 fusion.73
  498.8 36.7 %reduce-scatter.9.cloned.1.call-done = f32[96,2304]{1,0:T(8,128)} async-done(((f32[768,2304]{1,0:T(8,128)}), f32[96,2304]{1,0:T(8,128)}) %reduce-scatter.9.cloned.1.call-update) | async-done | bytes 884752 | tf_op jit(solution)/shard_map/reduce_scatter | solution.py:243
  537.5 130.3 %reduce-scatter.5.cloned.1.call-done = f32[96,2304]{1,0:T(8,128)} async-done(((f32[768,2304]{1,0:T(8,128)}), f32[96,2304]{1,0:T(8,128)}) %reduce-scatter.5.cloned.1.call-update) | async-done | bytes 884752 | tf_op jit(solution)/shard_map/reduce_scatter | solution.py:271
  669.8 5.6 add_convert_fusion
  678.0 31.1 %all-reduce.18.cloned.1.call-done = (bf16[96,2304]{1,0:T(8,128)(2,1)}, bf16[96,768]{1,0:T(8,128)(2,1)}, bf16[96,2304]{1,0:T(8,128)(2,1)}, bf16[144,768]{1,0:T(8,128)(2,1)}) async-done(((bf16[96,2304]{1,0:T(8,128)(2,1)}, bf16[96,768]{1,0:T(8,128)(2,1)}, bf16[96,2304]{1,0:T(8,128)(2,1)}, bf16[144,768]{1,0:T(8,128)(2,1)}), (bf16[96,2304]{1,0:T(8,128)(2,1)}, bf16[96,768]{1,0:T(8,128)(2,1)}, ...) | async-done | bytes 1253392 | tf_op jit(solution)/shard_map/psum | solution.py:276
  (295 shorter events, 221.4 us)
Async XLA Ops:
  7.2 71.2 %all-gather.5.cloned.1.call-start = ((), (), s32[]{:S(2)}) async-start(), calls=%async_computation.4 | async-start | bytes 3981312 | tf_op jit(solution)/shard_map/all_gather | solution.py:184
  7.9 201.3 %all-gather.7.cloned.1.call-start = ((), (), s32[]{:S(2)}) async-start(), calls=%async_computation.5 | async-start | bytes 1327104 | tf_op jit(solution)/shard_map/all_gather | solution.py:185
  8.6 206.0 %all-gather.9.cloned.1.call-start = ((), (), s32[]{:S(2)}) async-start(), calls=%async_computation.6 | async-start | bytes 3981312 | tf_op jit(solution)/shard_map/all_gather | solution.py:189
  9.4 223.4 %all-gather.11.cloned.1.call-start = ((), (), s32[]{:S(2)}) async-start(), calls=%async_computation.7 | async-start | bytes 1990656 | tf_op jit(solution)/shard_map/all_gather | solution.py:190
  10.0 485.3 %reduce-scatter.7.cloned.1.call-start = ((), (), s32[]{:S(2)}) async-start(), calls=%async_computation.9 | async-start | bytes 2654208 | tf_op jit(solution)/shard_map/reduce_scatter | solution.py:272
  10.1 2.6 copy-start.30
  10.1 3.9 copy-start.33
  10.1 4.1 copy-start.34
  11.9 197.4 %copy-start.1 = (bf16[1024,768]{0,1:T(8,128)(2,1)}, bf16[1024,768]{0,1:T(8,128)(2,1)S(1)}, u32[]{:S(2)}) copy-start(bf16[1024,768]{0,1:T(8,128)(2,1)S(1)} %copy.59) | copy-start | bytes 4718596
  12.1 66.2 %copy-start.23 = (f32[1024]{0:T(1024)}, f32[1024]{0:T(1024)S(1)}, u32[]{:S(2)}) copy-start(f32[1024]{0:T(1024)S(1)} %broadcast_multiply_fusion.8) | copy-start | bytes 12292
  12.6 71.7 %copy-start.25 = (f32[1024]{0:T(1024)}, f32[1024]{0:T(1024)S(1)}, u32[]{:S(2)}) copy-start(f32[1024]{0:T(1024)S(1)} %add_rsqrt_fusion.1) | copy-start | bytes 12292
  37.9 46.5 %copy-start.27 = (f32[768]{0:T(1024)}, f32[768]{0:T(1024)S(1)}, u32[]{:S(2)}) copy-start(f32[768]{0:T(1024)S(1)} %convert_element_type.157) | copy-start | bytes 9220
  39.0 51.3 %copy-start.16 = (f32[1024,64]{0,1:T(8,128)}, f32[1024,64]{0,1:T(8,128)S(1)}, u32[]{:S(2)}) copy-start(f32[1024,64]{0,1:T(8,128)S(1)} %get-tuple-element.338) | copy-start | bytes 786436
  39.0 51.3 %copy-start.18 = (f32[1024,64]{0,1:T(8,128)}, f32[1024,64]{0,1:T(8,128)S(1)}, u32[]{:S(2)}) copy-start(f32[1024,64]{0,1:T(8,128)S(1)} %get-tuple-element.339) | copy-start | bytes 786436
  97.3 2.6 slice-start
  100.0 4.1 copy-start.9
  123.2 1.7 copy-start.12
  212.5 1.7 copy-start.4
  214.7 18.2 %copy-start.20 = (bf16[1024,768]{1,0:T(8,128)(2,1)S(1)}, bf16[1024,768]{1,0:T(8,128)(2,1)}, u32[]{:S(2)}) copy-start(bf16[1024,768]{1,0:T(8,128)(2,1)} %param.19) | copy-start | bytes 4718596
  232.8 9.2 %copy-start.5 = (f32[1024,768]{0,1:T(8,128)S(1)}, f32[1024,768]{0,1:T(8,128)}, u32[]{:S(2)}) copy-start(f32[1024,768]{0,1:T(8,128)} %copy-done.4) | copy-start | bytes 9437188
  232.8 9.2 %copy-start.31 = (bf16[768,2304]{1,0:T(8,128)(2,1)S(1)}, bf16[768,2304]{1,0:T(8,128)(2,1)}, u32[]{:S(2)}) copy-start(bf16[768,2304]{1,0:T(8,128)(2,1)} %all-gather.9.cloned.1.call-done) | copy-start | bytes 10616836
  242.0 4.9 copy-start.35
  242.0 4.9 copy-start.36
  242.1 4.9 copy-start.11
  247.0 2.7 copy-start.21
  248.0 1.7 copy-start.8
  252.6 244.5 %reduce-scatter.11.cloned.1.call-start = ((), (), s32[]{:S(2)}) async-start(), calls=%async_computation.11 | async-start | bytes 3981312 | tf_op jit(solution)/shard_map/reduce_scatter | solution.py:244
  258.1 1.4 copy-start.32
  258.1 277.4 %reduce-scatter.9.cloned.1.call-start = ((), (), s32[]{:S(2)}) async-start(), calls=%async_computation.10 | async-start | bytes 7962624 | tf_op jit(solution)/shard_map/reduce_scatter | solution.py:243
  268.1 2.4 copy-start.6
  279.8 388.0 %reduce-scatter.5.cloned.1.call-start = ((), (), s32[]{:S(2)}) async-start(), calls=%async_computation.8 | async-start | bytes 7962624 | tf_op jit(solution)/shard_map/reduce_scatter | solution.py:271
  381.9 2.8 copy-start.14
  401.2 2.8 copy-start.15
  432.5 4.1 copy-start
  432.5 4.5 copy-start.10
  432.5 4.5 copy-start.19
  439.3 1.9 copy-start.3
  439.3 1.9 copy-start.17
  443.1 2.7 copy-start.2
  443.1 2.7 copy-start.24
  443.1 2.7 copy-start.26
  443.1 2.7 copy-start.28
  443.7 2.1 copy-start.13
  452.2 256.9 %all-reduce.18.cloned.1.call-start = ((), (), s32[]{:S(2)}) async-start(), calls=%async_computation.12 | async-start | bytes 2506752 | tf_op jit(solution)/shard_map/psum | solution.py:276
  452.8 9.3 %copy-start.29 = (f32[768]{0:T(1024)S(1)}, f32[768]{0:T(1024)}, u32[]{:S(2)}) copy-start(f32[768]{0:T(1024)} %get-tuple-element.262) | copy-start | bytes 9220
  495.3 174.5 %copy-start.7 = (f32[1024,768]{0,1:T(8,128)S(1)}, f32[1024,768]{0,1:T(8,128)}, u32[]{:S(2)}) copy-start(f32[1024,768]{0,1:T(8,128)} %copy-done.4) | copy-start | bytes 9437188
  709.0 5.7 copy-start.22
Sparse Core Ops, SparseCore 0:
  10.2 68.1 all-gather.4
  80.5 39.5 all-gather.6
  122.3 63.9 all-gather.8
  188.3 44.4 all-gather.10
  252.7 68.0 reduce-scatter.6
  324.2 78.1 reduce-scatter.10
  406.1 129.3 reduce-scatter.8
  539.6 128.0 reduce-scatter.4
  671.0 38.0 all-reduce.17
where the time goes:
time: 734 us; the launch traced here: 722 us
  waiting for transfers between devices  240 us (33%)
  matrix products  179 us (24%)
  local copies, waits for them, and re-layouts  142 us (19%)
  other arithmetic  86 us (12%)
  blocking collectives  50 us (7%)
  between operations  16 us (2%)
  loops' own time  8.62 us (1%)
    reduce_scatter x1, waiting for transfers between devices, body(): lax.psum_scatter(attn_members[1], 'shard', scatter_dimension=0, tiled=True)  130 us
    unnamed x2, blocking collectives  43.8 us
    reduce_scatter x1, waiting for transfers between devices, body(): lax.psum_scatter(ffn_members[1], 'shard', scatter_dimension=0, tiled=True)  36.7 us
    all_gather x1, waiting for transfers between devices, body(): lax.all_gather(w_qkv, 'shard', axis=0, tiled=True)  31.9 us
    psum x1, waiting for transfers between devices, body(): lax.psum(owned_qkv.astype(jnp.bfloat16), 'replica').astype(jnp.float32)  31.1 us
    dot_general x12, matrix products, block_scores(): jnp.einsum('qhd,khd->hqk', query_part, key_part, preferred_element_type=j...  24.6 us
    unnamed x86, local copies, waits for them, and re-layouts  21.1 us
    dot_general x6, matrix products, one_block(): jnp.einsum('hqk,khd->qhd', probs, value_part, preferred_element_type=jnp....  20.8 us
  transfers between devices with their start and end apart: 9, of which 5 were waited for; matrix products, arithmetic and copies ran while one was open for 51% of the time, Pallas kernels for 0%

commit v1 on v0

--- a/solution.py
+++ b/solution.py
@@ -3,6 +3,7 @@
 import jax.numpy as jnp
 from jax import lax
 from jax.sharding import PartitionSpec as P
+from jax.lax import axis_index, axis_size, ppermute
 
 D = 768
 HEADS = 12
@@ -179,9 +180,24 @@
 
 def body(tokens, gain_attn, w_qkv, w_out, gain_ffn, w_in, w_down, cotangent):
     count_tok = tokens.shape[0]
+
+    def review_the_boxes(obj, ndim_at=0):
+        raw_out, local_out = (axis_size("shard"), axis_index("shard"))
+        s_next, later = (obj, 1)
+        while later < raw_out:
+            series = []
+            for at in range(raw_out):
+                series.append((at, at ^ later))
+            heard = ppermute(s_next, "shard", perm=series)
+            answer = jnp.concatenate([s_next, heard], axis=ndim_at)
+            reached = jnp.concatenate([heard, s_next], axis=ndim_at)
+            s_next = jnp.where(local_out & later == 0, answer, reached)
+            later = 2 * later
+        return s_next
+
     gain_one, joint_weight, out_weight = (
         lax.all_gather(gain_attn, "shard", axis=0, tiled=True),
-        lax.all_gather(w_qkv, "shard", axis=0, tiled=True),
+        review_the_boxes(w_qkv),
         lax.all_gather(w_out, "shard", axis=0, tiled=True),
     )
     gain_two, in_weight, down_weight = (

time: 734 us -> 836 us (1.14)
  waiting for transfers between devices: 240 us -> 321 us
  blocking collectives: 50 us -> 67.1 us
    ppermute x0 -> x3, waiting for transfers between devices: none -> 120 us  [review_the_boxes(): heard = ppermute(s_next, 'shard', perm=series)]
    all_gather x1, waiting for transfers between devices: 31.9 us -> 0.02 us  [body(): lax.all_gather(w_qkv, 'shard', axis=0, tiled=True)]
    unnamed x2, blocking collectives: 43.8 us -> 60.9 us
  transfers between devices with their start and end apart: 9 -> 12, of which waited for: 5 -> 5; matrix products, arithmetic and copies ran while one was open for 51% -> 47% of each run, Pallas kernels for 0% -> 0%
where the time goes in v1:
time: 836 us; the launch traced here: 824 us
  waiting for transfers between devices  321 us (38%)
  matrix products  177 us (21%)
  local copies, waits for them, and re-layouts  141 us (17%)
  other arithmetic  87.9 us (11%)
  blocking collectives  67.1 us (8%)
  between operations  16.1 us (2%)
  loops' own time  8.62 us (1%)
    reduce_scatter x1, waiting for transfers between devices, body(): lax.psum_scatter(attn_members[1], 'shard', scatter_dimension=0, tiled=True)  130 us
    ppermute x3, waiting for transfers between devices, review_the_boxes(): heard = ppermute(s_next, 'shard', perm=series)  120 us
    unnamed x2, blocking collectives  60.9 us
    reduce_scatter x1, waiting for transfers between devices, body(): lax.psum_scatter(ffn_members[1], 'shard', scatter_dimension=0, tiled=True)  37.5 us
    psum x1, waiting for transfers between devices, body(): lax.psum(owned_qkv.astype(jnp.bfloat16), 'replica').astype(jnp.float32)  31.1 us
    dot_general x12, matrix products, block_scores(): jnp.einsum('qhd,khd->hqk', query_part, key_part, preferred_element_type=j...  24.6 us
    unnamed x86, local copies, waits for them, and re-layouts  20.9 us
    dot_general x6, matrix products, one_block(): jnp.einsum('hqk,khd->qhd', probs, value_part, preferred_element_type=jnp....  20.8 us
  transfers between devices with their start and end apart: 12, of which 5 were waited for; matrix products, arithmetic and copies ran while one was open for 47% of the time, Pallas kernels for 0%

profile of v1, /device:TPU:0, one launch (start us, length us, event | category | flops | bytes accessed | tf_op | source)
XLA Modules:
  0.0 823.9 jit_solution(1509550396945749144)
XLA Ops:
  12.5 11.1 %collective-permute-done = bf16[96,2304]{1,0:T(8,128)(2,1)S(1)} collective-permute-done((bf16[96,2304]{1,0:T(8,128)(2,1)}, bf16[96,2304]{1,0:T(8,128)(2,1)S(1)}, u32[]{:S(2)}, u32[]{:S(2)}) %collective-permute-start) | collective-permute-done | bytes 442400 | tf_op jit(solution)/shard_map/ppermute | solution.py:191
  30.1 40.6 %all-reduce.13 = (bf16[768]{0:T(1024)(128)(2,1)S(1)}, bf16[768]{0:T(1024)(128)(2,1)S(1)}) all-reduce(bf16[768]{0:T(1024)(128)(2,1)S(1)} %dynamic-update-slice, bf16[768]{0:T(1024)(128)(2,1)S(1)} %dynamic-update-slice.1), channel_id=1, replica_groups=mesh['replica'=4,'shard'=8] {'shard'}, use_global_device_ids=true, to_apply=%add.8 | all-reduce | flops 1536 | bytes 6144
  75.3 4.4 fusion.107
  80.5 108.6 %collective-permute-done.2 = bf16[384,2304]{1,0:T(8,128)(2,1)S(1)} collective-permute-done((bf16[384,2304]{1,0:T(8,128)(2,1)S(1)}, bf16[384,2304]{1,0:T(8,128)(2,1)S(1)}, u32[]{:S(2)}, u32[]{:S(2)}) %collective-permute-start.2) | collective-permute-done | bytes 1769504 | tf_op jit(solution)/shard_map/ppermute | solution.py:191
  189.1 4.0 fusion.68
  193.1 4.1 slice_bitcast_fusion
  202.1 3.8 reshape.520
  208.8 3.7 maximum_bitcast_fusion.1
  214.9 3.4 concatenate.115
  218.3 3.4 concatenate.116
  221.7 5.6 squeeze.70
  227.3 4.7 fusion.97
  236.7 3.9 reshape.516
  242.7 3.9 concatenate.111
  246.6 3.7 maximum_bitcast_fusion
  252.0 61.0 %while.30 = (s32[]{:T(128)}, bf16[6,512,4,64]{1,3,2,0:T(8,128)(2,1)}, f32[6,4,512]{2,1,0:T(4,128)}, bf16[6,640,4,64]{1,3,2,0:T(8,128)(2,1)}, s32[6]{0:T(128)S(1)...) while((s32[]{:T(128)}, ...), condition=%wide.region_5.6_spmd, body=%wide.region_2.5_spmd.sunk | while | flops 352716416 | bytes 18297728 | solution.py:132
  258.6 3.5 fusion.160
  268.8 3.5 fusion.160
  278.9 3.5 fusion.160
  289.1 3.5 fusion.160
  299.2 3.5 fusion.160
  309.4 3.5 fusion.160
  323.1 10.6 %fusion.117 = f32[1024,2304]{1,0:T(8,128)} fusion(bf16[768,2304]{1,0:T(8,128)(2,1)} %all-gather.7.cloned.1.call-done, f32[1024,768]{0,1:T(8,128)} %copy-done.4, f32[768]{0:T(1024)S(1)} %convert_element_type.164, f32[1024]{0:T(1024)S(1)} %add_rsqrt_fusion, f32[1024]{0:T(1024)S(1)} %broadcast_multiply_fusion.7), kind=kOutput, calls=%fused_computation.197 | convolution fusion | flops 3627024384 | bytes 16133120 | tf_op jit(solution)/shard_map/dot_general | solution.py:223
  333.7 9.2 %fusion.61 = (bf16[1024,1152]{1,0:T(8,128)(2,1)S(1)}, bf16[1024,1152]{1,0:T(8,128)(2,1)S(1)}, bf16[1024,1152]{1,0:T(8,128)(2,1)}) fusion(f32[1024,2304]{1,0:T(8,128)} %fusion.117, bf16[1024,768]{1,0:T(8,128)(2,1)S(1)} %copy-done.20, bf16[1152,768]{1,0:T(8,128)(2,1)} %all-gather.9.cloned.1.call-done), kind=kOutput, calls=%fused_computation.78 | convolution fusion | flops 1830813696 | bytes 19857408 | tf_op jit(solution)/shard_map/td,fd->tf/dot_general | solution.py:243
  343.0 4.9 multiply_reduce_fusion.1
  353.5 5.5 fusion.120
  360.4 4.5 convolution_convert_fusion
  371.4 9.3 %fusion.90 = f32[768,2304]{1,0:T(8,128)} fusion(bf16[1024,1152]{1,0:T(8,128)(2,1)} %copy-done.36, bf16[1024,1152]{1,0:T(8,128)(2,1)} %copy-done.35, f32[1024,768]{0,1:T(8,128)S(1)} %copy-done.6, f32[768]{0:T(1024)S(1)} %convert_element_type.164, f32[1024]{0:T(1024)S(1)} %add_rsqrt_fusion, f32[1024]{0:T(1024)S(1)} %broadcast_multiply_fusion.7), kind=kOutput, calls=%fused_computation.131 | convolution fusion | flops 3636461568 | bytes 14953472 | tf_op jit(solution)/shard_map/td,te->de/dot_general | solution.py:248
  380.7 95.8 %while.31 = (s32[]{:T(128)}, f32[6,512,4,64]{1,3,2,0:T(8,128)}, f32[6,640,4,64]{1,3,2,0:T(8,128)}, f32[6,640,4,64]{1,3,2,0:T(8,128)}, bf16[6,640,4,64]{1,3,2,0:T...) while((s32[]{:T(128)}, f32[6,512,4,64]{1,3,2,0:T(8,128)}, ...), condition=%wide.region_12.13_spmd, body=%wide.region_10.12_spmd.sunk | while | flops 860128896 | bytes 44572060 | solution.py:172
  476.5 5.2 copy.70
  488.0 3.8 reshape_reshape.26
  491.8 3.9 reshape_reshape.25
  495.8 5.2 copy.71
  507.8 4.3 reshape.527
  512.1 5.6 reshape.526
  517.7 4.0 pad.36
  521.7 5.6 reshape.532
  527.3 6.0 reshape.531
  533.4 4.1 fusion.93
  546.8 6.2 fusion.101
  553.8 9.3 %fusion.81 = (f32[768]{0:T(1024)S(1)}, f32[1024]{0:T(1024)S(1)}, f32[1024]{0:T(1024)S(1)}, f32[1024,768]{0,1:T(8,128)}) fusion(bf16[1024,768]{0,1:T(8,128)(2,1)S(1)} %copy-done.2, f32[1024]{0:T(1024)S(1)} %copy-done.28, f32[1024]{0:T(1024)S(1)} %copy-done.24, f32[768]{0:T(1024)S(1)} %copy-done.26, bf16[768,2304]{1,0:T(8,128)(2,1)} %all-gather.11.cloned.1.call-done, ...), kind=kOutput, calls=%fused_computation.105 | convolution fusion | flops 3630953728 | bytes 12998656 | tf_op jit(solution)/shard_map/te,de->td/dot_general | solution.py:277
  563.1 20.2 %all-reduce.12 = (bf16[768]{0:T(1024)(128)(2,1)S(1)}, bf16[768]{0:T(1024)(128)(2,1)S(1)}) all-reduce(f32[768]{0:T(1024)S(1)} %get-tuple-element.264, f32[768]{0:T(1024)S(1)} %copy-done.29), channel_id=2, replica_groups=mesh['replica'=4,'shard'=8] {'shard'}, use_global_device_ids=true, to_apply=%region_16.17.clone | all-reduce | flops 1536 | bytes 9216
  583.5 6.2 all-reduce.14
  590.7 3.9 fusion.80
  599.7 37.5 %reduce-scatter.9.cloned.1.call-done = f32[96,2304]{1,0:T(8,128)} async-done(((f32[768,2304]{1,0:T(8,128)}), f32[96,2304]{1,0:T(8,128)}) %reduce-scatter.9.cloned.1.call-update) | async-done | bytes 884752 | tf_op jit(solution)/shard_map/reduce_scatter | solution.py:259
  639.2 130.3 %reduce-scatter.5.cloned.1.call-done = f32[96,2304]{1,0:T(8,128)} async-done(((f32[768,2304]{1,0:T(8,128)}), f32[96,2304]{1,0:T(8,128)}) %reduce-scatter.5.cloned.1.call-update) | async-done | bytes 884752 | tf_op jit(solution)/shard_map/reduce_scatter | solution.py:287
  771.5 5.6 add_convert_fusion
  779.6 31.1 %all-reduce.18.cloned.1.call-done = (bf16[96,2304]{1,0:T(8,128)(2,1)}, bf16[96,768]{1,0:T(8,128)(2,1)}, bf16[96,2304]{1,0:T(8,128)(2,1)}, bf16[144,768]{1,0:T(8,128)(2,1)}) async-done(((bf16[96,2304]{1,0:T(8,128)(2,1)}, bf16[96,768]{1,0:T(8,128)(2,1)}, bf16[96,2304]{1,0:T(8,128)(2,1)}, bf16[144,768]{1,0:T(8,128)(2,1)}), (bf16[96,2304]{1,0:T(8,128)(2,1)}, bf16[96,768]{1,0:T(8,128)(2,1)}, ...) | async-done | bytes 1253392 | tf_op jit(solution)/shard_map/psum | solution.py:292
  (303 shorter events, 227.4 us)
Async XLA Ops:
  7.2 21.1 %copy-start.30 = (u32[32]{0:T(128)S(1)}, u32[32]{0:T(128)}, u32[]{:S(2)}) copy-start(u32[32]{0:T(128)} %constant.216) | copy-start | bytes 388
  7.2 22.5 %copy-start.33 = (bf16[96]{0:T(256)(128)(2,1)S(1)}, bf16[96]{0:T(256)(128)(2,1)}, u32[]{:S(2)}) copy-start(bf16[96]{0:T(256)(128)(2,1)} %param.13) | copy-start | bytes 580
  7.2 22.7 %copy-start.34 = (bf16[96]{0:T(256)(128)(2,1)S(1)}, bf16[96]{0:T(256)(128)(2,1)}, u32[]{:S(2)}) copy-start(bf16[96]{0:T(256)(128)(2,1)} %param.16) | copy-start | bytes 580
  7.2 310.4 %all-gather.5.cloned.1.call-start = ((), (), s32[]{:S(2)}) async-start(), calls=%async_computation.4 | async-start | bytes 1327104 | tf_op jit(solution)/shard_map/all_gather | solution.py:201
  7.9 315.1 %all-gather.7.cloned.1.call-start = ((), (), s32[]{:S(2)}) async-start(), calls=%async_computation.5 | async-start | bytes 3981312 | tf_op jit(solution)/shard_map/all_gather | solution.py:205
  8.7 325.0 %all-gather.9.cloned.1.call-start = ((), (), s32[]{:S(2)}) async-start(), calls=%async_computation.6 | async-start | bytes 1990656 | tf_op jit(solution)/shard_map/all_gather | solution.py:206
  9.4 544.3 %all-gather.11.cloned.1.call-start = ((), (), s32[]{:S(2)}) async-start(), calls=%async_computation.7 | async-start | bytes 3981312 | tf_op jit(solution)/shard_map/all_gather | solution.py:233
  9.5 14.2 %collective-permute-start = (bf16[96,2304]{1,0:T(8,128)(2,1)}, bf16[96,2304]{1,0:T(8,128)(2,1)S(1)}, u32[]{:S(2)}, u32[]{:S(2)}) collective-permute-start(bf16[96,2304]{1,0:T(8,128)(2,1)} %param.14), channel_id=1, source_target_pairs={{0,1},{1,0},{2,3},{3,2},{4,5},{5,4},{6,7},{7,6},{8,9},{9,8},{10,11... | collective-permute-start | bytes 1327112 | tf_op jit(solution)/shard_map/ppermute | solution.py:191
  25.0 48.5 %collective-permute-start.1 = (bf16[192,2304]{1,0:T(8,128)(2,1)S(1)}, bf16[192,2304]{1,0:T(8,128)(2,1)S(1)}, u32[]{:S(2)}, u32[]{:S(2)}) collective-permute-start(bf16[192,2304]{1,0:T(8,128)(2,1)S(1)} %maximum_select_fusion.3), channel_id=1, source_target_pairs={{0,2},{1,3},{2,0},{3,1},{4,6},{5,7},{6,4},{7,5},{8,10},{9,11},{10,... | collective-permute-start | bytes 2654216 | tf_op jit(solution)/shard_map/ppermute | solution.py:191
  26.4 569.8 %reduce-scatter.7.cloned.1.call-start = ((), (), s32[]{:S(2)}) async-start(), calls=%async_computation.9 | async-start | bytes 2654208 | tf_op jit(solution)/shard_map/reduce_scatter | solution.py:288
  28.2 289.4 %copy-start.1 = (bf16[1024,768]{0,1:T(8,128)(2,1)}, bf16[1024,768]{0,1:T(8,128)(2,1)S(1)}, u32[]{:S(2)}) copy-start(bf16[1024,768]{0,1:T(8,128)(2,1)S(1)} %copy.59) | copy-start | bytes 4718596
  70.7 118.4 %copy-start.25 = (f32[768]{0:T(1024)}, f32[768]{0:T(1024)S(1)}, u32[]{:S(2)}) copy-start(f32[768]{0:T(1024)S(1)} %convert_element_type.157) | copy-start | bytes 9220
  74.0 115.0 %collective-permute-start.2 = (bf16[384,2304]{1,0:T(8,128)(2,1)S(1)}, bf16[384,2304]{1,0:T(8,128)(2,1)S(1)}, u32[]{:S(2)}, u32[]{:S(2)}) collective-permute-start(bf16[384,2304]{1,0:T(8,128)(2,1)S(1)} %maximum_select_fusion.2), channel_id=1, source_target_pairs={{0,4},{1,5},{2,6},{3,7},{4,0},{5,1},{6,2},{7,3},{8,12},{9,13},{10,... | collective-permute-start | bytes 5308424 | tf_op jit(solution)/shard_map/ppermute | solution.py:191
  75.2 123.7 %copy-start.16 = (f32[1024,64]{0,1:T(8,128)}, f32[1024,64]{0,1:T(8,128)S(1)}, u32[]{:S(2)}) copy-start(f32[1024,64]{0,1:T(8,128)S(1)} %get-tuple-element.338) | copy-start | bytes 786436
  75.2 123.7 %copy-start.18 = (f32[1024,64]{0,1:T(8,128)}, f32[1024,64]{0,1:T(8,128)S(1)}, u32[]{:S(2)}) copy-start(f32[1024,64]{0,1:T(8,128)S(1)} %get-tuple-element.339) | copy-start | bytes 786436
  80.0 113.1 %copy-start.23 = (f32[1024]{0:T(1024)}, f32[1024]{0:T(1024)S(1)}, u32[]{:S(2)}) copy-start(f32[1024]{0:T(1024)S(1)} %broadcast_multiply_fusion.8) | copy-start | bytes 12292
  80.5 112.6 %copy-start.27 = (f32[1024]{0:T(1024)}, f32[1024]{0:T(1024)S(1)}, u32[]{:S(2)}) copy-start(f32[1024]{0:T(1024)S(1)} %add_rsqrt_fusion.1) | copy-start | bytes 12292
  206.0 2.8 slice-start
  208.8 4.1 copy-start.9
  232.1 1.7 copy-start.12
  320.9 1.8 copy-start.4
  323.0 10.7 %copy-start.20 = (bf16[1024,768]{1,0:T(8,128)(2,1)S(1)}, bf16[1024,768]{1,0:T(8,128)(2,1)}, u32[]{:S(2)}) copy-start(bf16[1024,768]{1,0:T(8,128)(2,1)} %param.19) | copy-start | bytes 4718596
  333.7 9.2 %copy-start.5 = (f32[1024,768]{0,1:T(8,128)S(1)}, f32[1024,768]{0,1:T(8,128)}, u32[]{:S(2)}) copy-start(f32[1024,768]{0,1:T(8,128)} %copy-done.4) | copy-start | bytes 9437188
  333.7 9.2 %copy-start.31 = (bf16[768,2304]{1,0:T(8,128)(2,1)S(1)}, bf16[768,2304]{1,0:T(8,128)(2,1)}, u32[]{:S(2)}) copy-start(bf16[768,2304]{1,0:T(8,128)(2,1)} %all-gather.7.cloned.1.call-done) | copy-start | bytes 10616836
  342.9 4.9 copy-start.35
  342.9 4.9 copy-start.36
  343.0 4.9 copy-start.11
  347.9 2.7 copy-start.21
  353.5 244.4 %reduce-scatter.11.cloned.1.call-start = ((), (), s32[]{:S(2)}) async-start(), calls=%async_computation.11 | async-start | bytes 3981312 | tf_op jit(solution)/shard_map/reduce_scatter | solution.py:260
  359.0 278.2 %reduce-scatter.9.cloned.1.call-start = ((), (), s32[]{:S(2)}) async-start(), calls=%async_computation.10 | async-start | bytes 7962624 | tf_op jit(solution)/shard_map/reduce_scatter | solution.py:259
  368.9 2.4 copy-start.6
  380.7 388.8 %reduce-scatter.5.cloned.1.call-start = ((), (), s32[]{:S(2)}) async-start(), calls=%async_computation.8 | async-start | bytes 7962624 | tf_op jit(solution)/shard_map/reduce_scatter | solution.py:287
  482.8 2.8 copy-start.14
  502.1 2.8 copy-start.15
  533.4 4.1 copy-start
  533.4 4.5 copy-start.10
  533.4 4.5 copy-start.19
  540.2 1.9 copy-start.3
  540.2 1.9 copy-start.17
  544.0 2.8 copy-start.2
  544.0 2.7 copy-start.24
  544.0 2.7 copy-start.26
  544.1 2.7 copy-start.28
  544.6 2.1 copy-start.13
  553.0 257.7 %all-reduce.18.cloned.1.call-start = ((), (), s32[]{:S(2)}) async-start(), calls=%async_computation.12 | async-start | bytes 2506752 | tf_op jit(solution)/shard_map/psum | solution.py:292
  553.7 9.3 %copy-start.29 = (f32[768]{0:T(1024)S(1)}, f32[768]{0:T(1024)}, u32[]{:S(2)}) copy-start(f32[768]{0:T(1024)} %get-tuple-element.262) | copy-start | bytes 9220
  596.1 175.3 %copy-start.7 = (f32[1024,768]{0,1:T(8,128)S(1)}, f32[1024,768]{0,1:T(8,128)}, u32[]{:S(2)}) copy-start(f32[1024,768]{0,1:T(8,128)} %copy-done.4) | copy-start | bytes 9437188
  810.7 5.7 copy-start.22
  (2 other events, 3.0 us)
Sparse Core Ops, SparseCore 0:
  10.2 49.0 all-gather.4
  61.5 119.7 all-gather.6
  183.6 44.8 all-gather.8
  230.5 64.1 all-gather.10
  353.6 67.9 reduce-scatter.6
  425.1 78.2 reduce-scatter.10
  507.1 130.1 reduce-scatter.8
  641.3 128.0 reduce-scatter.4
  772.7 38.0 all-reduce.17
